TPU v7x, 32 devices: a whole 2x2x4 slice. The times are simulated.
32 devices in a mesh: parts: 2 (over y), wide: 8 (over z, x), narrow: 2 (over core).
Axes of the slice: x: 2, y: 2, z: 4, core: 2. Of those that a mesh axis runs over, the one named last changes fastest.
Arguments:
- state: float32 [128, 64, 256], P(('parts', 'wide'), 'narrow'), parts along dimension 0, may hold values from -6 to 6
- permeability: float32 [128, 64, 256], P(('parts', 'wide'), 'narrow'), parts along dimension 0, may hold values from 0.3 to 3
- direction: float32 [128, 64, 256], P(('parts', 'wide'), 'narrow'), parts along dimension 0, may hold values from -6 to 6
- obs_weight: float32 [128, 64, 256], P(('parts', 'wide'), 'narrow'), parts along dimension 0, may hold values from 0.5 to 5
- coarse_inverse: float32 [32, 16], P('parts'), parts along dimension 0, as said below
Outputs:
- hessian_action: float32 [128, 64, 256], P(('parts', 'wide'), 'narrow'), parts along dimension 0
- increment: float32 [128, 64, 256], P(('parts', 'wide'), 'narrow'), parts along dimension 0
There are 2 independent parts, one for each index of `parts`. A program takes and returns all parts, laid end to end along the dimension named above; each array names one. Nothing has to cross between parts.
Inputs may be any that keep to these rules, and one draw needn't show every extreme that they name: `coarse_inverse`: a given dense matrix over bricks, not derived from the permeability.
All inputs are finite; a program needn't handle non-finite values.
Results may differ from a plain program's by a relative error of at most 0.0003.
Values sent between devices are 32-bit elements; how exact they have to be, the bound alone decides.
A program may use at most 128 MiB of HBM per device.

v0:
```python
import jax
import jax.numpy as jnp
from jax import lax
from jax.sharding import PartitionSpec as P

cheb_mid = 1.125
cheb_half = 0.875
first_rho = cheb_half / cheb_mid
second_rho = 1.0 / (2.0 * cheb_mid / cheb_half - first_rho)
step_gain = 2.0 * second_rho / cheb_half
carry_gain = second_rho * first_rho


def padded_2(cells, sides, width):
    for axis, dim in sides:
        count = lax.axis_size(axis)
        ends = count - 1
        head = lax.slice_in_dim(cells, 0, width, axis=dim)
        tail = lax.slice_in_dim(cells, cells.shape[dim] - width, cells.shape[dim], axis=dim)
        cells = jnp.concatenate(
            [
                lax.ppermute(tail, axis, [(i, (i + 1) % count) for i in range(ends)]),
                cells,
                lax.ppermute(head, axis, [((i + 1) % count, i) for i in range(ends)]),
            ],
            axis=dim,
        )
    return cells


def pad_depth(values):
    return jnp.pad(values, ((0, 0), (0, 0), (1, 1)))


def neighbour_list(padded):
    middle = padded[1:-1, 1:-1]
    deeper = pad_depth(middle)
    return (
        middle,
        [
            padded[2:, 1:-1],
            padded[:-2, 1:-1],
            padded[1:-1, 2:],
            padded[1:-1, :-2],
            deeper[:, :, 2:],
            deeper[:, :, :-2],
        ],
    )


def apply_pad(padded, coeff_pad, factor):
    middle, beside_all = neighbour_list(padded)
    own_coeff, coeff_around = neighbour_list(coeff_pad)
    summed = jnp.zeros_like(middle)
    for beside, beside_coeff in zip(beside_all, coeff_around):
        summed = summed + 0.5 * (own_coeff + beside_coeff) * (middle - beside)
    return factor * summed


def diagonal_pad(coeff_pad, factor):
    own_coeff, coeff_around = neighbour_list(coeff_pad)
    summed = jnp.zeros_like(own_coeff)
    for beside_coeff in coeff_around:
        summed = summed + 0.5 * (own_coeff + beside_coeff)
    return factor * summed


def hessian_pad(state_pad, adjoint_pad, permeability):
    state_mid, state_around = neighbour_list(state_pad)
    adjoint_mid, adjoint_around = neighbour_list(adjoint_pad)
    summed = jnp.zeros_like(state_mid)
    for state_side, adjoint_side in zip(state_around, adjoint_around):
        summed = summed + (state_mid - state_side) * (adjoint_mid - adjoint_side)
    return 0.5 * permeability * summed


def coarsen(values):
    first, second, third = values.shape
    return values.reshape(first // 2, 2, second // 2, 2, third // 2, 2).mean(axis=(1, 3, 5))


def refine(values):
    return jnp.repeat(jnp.repeat(jnp.repeat(values, 2, 0), 2, 1), 2, 2)


def smooth_zero(target, operate, inverse_diag):
    update = inverse_diag * target / cheb_mid
    iterate = update
    resid = target - operate(iterate)
    update = carry_gain * update + step_gain * inverse_diag * resid
    return iterate + update


def smooth_from(start, target, operate, inverse_diag):
    resid = target - operate(start)
    update = inverse_diag * resid / cheb_mid
    iterate = start + update
    resid = target - operate(iterate)
    update = carry_gain * update + step_gain * inverse_diag * resid
    return iterate + update


def shards(state, permeability, direction, obs_weight, coarse_inverse):
    depth = state.shape[2]
    stacked = jnp.concatenate([state, permeability, direction, obs_weight], axis=2)
    stacked_pad = padded_2(stacked, (("wide", 0), ("narrow", 1)), 2)
    state_pad = stacked_pad[:, :, :depth]
    k_pad_two = stacked_pad[:, :, depth : 2 * depth]
    dir_pad = stacked_pad[:, :, 2 * depth : 3 * depth]
    k_pad_one = k_pad_two[1:-1, 1:-1]
    coarse_k_pad = padded_2(coarsen(permeability), (("wide", 0), ("narrow", 1)), 1)
    inv_fine = 1.0 / diagonal_pad(k_pad_one, 1.0)
    inv_coarse = 1.0 / diagonal_pad(coarse_k_pad, 0.25)
    slot = lax.axis_index("wide") * lax.axis_size("narrow") + lax.axis_index("narrow")
    bricks = lax.axis_size("wide") * lax.axis_size("narrow")

    def pre_apply(values):
        return apply_pad(padded_2(values, (("wide", 0), ("narrow", 1)), 1), k_pad_one, 1.0)

    def fine_apply(values):
        return apply_pad(padded_2(values, (("wide", 0), ("narrow", 1)), 1), k_pad_one, 1.0)

    def post_apply(values):
        return apply_pad(padded_2(values, (("wide", 0), ("narrow", 1)), 1), k_pad_one, 1.0)

    def coarse_apply(values):
        return apply_pad(padded_2(values, (("wide", 0), ("narrow", 1)), 1), coarse_k_pad, 0.25)

    def vcycle(target):
        iterate = smooth_zero(target, pre_apply, inv_fine)
        coarse_target = coarsen(target - fine_apply(iterate))
        coarse_iter = smooth_zero(coarse_target, coarse_apply, inv_coarse)
        leftover = jnp.sum(coarse_target - coarse_apply(coarse_iter))
        slot_ids = jnp.arange(bricks, dtype=jnp.int32)
        totals = lax.psum(jnp.where(slot_ids == slot, leftover, 0.0), ("wide", "narrow"))
        inverse_row = lax.dynamic_slice_in_dim(coarse_inverse, slot, 1, 0)[0]
        correction = jnp.sum(inverse_row * totals)
        coarse_iter = smooth_from(coarse_iter + correction, coarse_target, coarse_apply, inv_coarse)
        iterate = iterate + refine(coarse_iter)
        return smooth_from(iterate, target, post_apply, inv_fine)

    source_ext = -apply_pad(state_pad, dir_pad * k_pad_two, 1.0)
    source = source_ext[1:-1, 1:-1]
    increment = vcycle(source)
    adjoint_source = -(obs_weight * increment)
    adjoint = vcycle(adjoint_source)
    adjoint_pad = padded_2(adjoint, (("wide", 0), ("narrow", 1)), 1)
    hessian = hessian_pad(state_pad[1:-1, 1:-1], adjoint_pad, permeability)
    return (hessian, increment)


def solution(mesh):
    placed = (
        P(("parts", "wide"), "narrow", None),
        P(("parts", "wide"), "narrow", None),
        P(("parts", "wide"), "narrow", None),
        P(("parts", "wide"), "narrow", None),
        P("parts", None),
    )
    return jax.shard_map(
        shards,
        mesh=mesh,
        in_specs=placed,
        out_specs=(P(("parts", "wide"), "narrow", None), P(("parts", "wide"), "narrow", None)),
        check_vma=False,
    )
```

profile of v0, /device:TPU:0, one launch (start us, length us, event | category | flops | bytes accessed | tf_op | source)
XLA Modules:
  0.0 453.2 jit_solution(4842753370702765318)
XLA Ops:
  5.9 5.5 %collective-permute-start.1 = (f32[2,32,1024]{2,1,0:T(8,128)S(1)}, f32[2,32,1024]{2,1,0:T(8,128)S(1)}, u32[]{:S(2)}, u32[]{:S(2)}) collective-permute-start(f32[2,32,1024]{2,1,0:T(8,128)S(1)} %get-tuple-element.34), channel_id=1, source_target_pairs={{0,2},{2,4},{4,6},{6,8},{8,10},{10,12},{12,14},{1,3},{3,5},{5,7},{... | collective-permute-start | bytes 786440 | tf_op jit(solution)/shard_map/ppermute | solution.py:22
  11.4 4.3 collective-permute-done
  15.8 5.8 %collective-permute-done.1 = f32[2,32,1024]{2,1,0:T(8,128)S(1)} collective-permute-done((f32[2,32,1024]{2,1,0:T(8,128)S(1)}, f32[2,32,1024]{2,1,0:T(8,128)S(1)}, u32[]{:S(2)}, u32[]{:S(2)}) %collective-permute-start.1) | collective-permute-done | bytes 262176 | tf_op jit(solution)/shard_map/ppermute | solution.py:22
  21.6 1.9 collective-permute-start.3
  30.4 4.4 collective-permute-start.5
  36.0 18.9 %reshape.31 = f32[4,2,16,2,128,2]{5,4,3,2,1,0:T(8,128)} reshape(f32[8,32,256]{2,1,0:T(8,128)} %param.6) | data formatting | bytes 524288 | tf_op jit(solution)/shard_map/reshape | solution.py:79
  54.9 7.6 %reduce_sum.63 = f32[4,16,128]{2,1,0:T(8,128)} reduce(f32[4,2,16,2,128,2]{5,4,3,2,1,0:T(8,128)} %reshape.31, f32[]{:T(128)} %constant.45.clone.1), dimensions={1,3,5}, to_apply=%region_0.0 | reduce | flops 57344 | bytes 294916 | tf_op jit(solution)/shard_map/reduce_sum | solution.py:79
  64.7 3.0 collective-permute-start.7
  68.6 2.6 fusion.16
  71.2 4.5 %collective-permute-start.13 = (f32[1,32,256]{2,1,0:T(8,128)S(1)}, f32[1,32,256]{2,1,0:T(8,128)S(1)}, u32[]{:S(2)}, u32[]{:S(2)}) collective-permute-start(f32[1,32,256]{2,1,0:T(8,128)S(1)} %get-tuple-element.74), channel_id=1, source_target_pairs={{0,2},{2,4},{4,6},{6,8},{8,10},{10,12},{12,14},{1,3},{3,5},{5,7},{... | collective-permute-start | bytes 98312 | tf_op jit(solution)/shard_map/ppermute | solution.py:22
  77.0 4.5 %collective-permute-start.9 = (f32[1,16,128]{2,1,0:T(8,128)S(1)}, f32[1,16,128]{2,1,0:T(8,128)S(1)}, u32[]{:S(2)}, u32[]{:S(2)}) collective-permute-start(f32[1,16,128]{2,1,0:T(8,128)S(1)} %get-tuple-element.112), channel_id=1, source_target_pairs={{0,2},{2,4},{4,6},{6,8},{8,10},{10,12},{12,14},{1,3},{3,5},{5,7},{... | collective-permute-start | bytes 24584 | tf_op jit(solution)/shard_map/ppermute | solution.py:22
  84.2 3.0 collective-permute-start.15
  92.3 18.9 %reshape.32 = f32[4,2,16,2,128,2]{5,4,3,2,1,0:T(8,128)} reshape(f32[8,32,256]{2,1,0:T(8,128)} %fusion.23) | data formatting | bytes 524288 | tf_op jit(solution)/shard_map/reshape | solution.py:79
  111.1 7.0 %reduce_sum.64 = f32[4,16,128]{2,1,0:T(8,128)S(1)} reduce(f32[4,2,16,2,128,2]{5,4,3,2,1,0:T(8,128)} %reshape.32, f32[]{:T(128)} %constant.45.clone.1), dimensions={1,3,5}, to_apply=%region_1.2 | reduce | flops 57344 | bytes 294916 | tf_op jit(solution)/shard_map/reduce_sum | solution.py:79
  118.9 4.8 %collective-permute-start.17 = (f32[1,16,128]{2,1,0:T(8,128)S(1)}, f32[1,16,128]{2,1,0:T(8,128)S(1)}, u32[]{:S(2)}, u32[]{:S(2)}) collective-permute-start(f32[1,16,128]{2,1,0:T(8,128)S(1)} %get-tuple-element.110), channel_id=1, source_target_pairs={{0,2},{2,4},{4,6},{6,8},{8,10},{10,12},{12,14},{1,3},{3,5},{5,7},{... | collective-permute-start | bytes 24584 | tf_op jit(solution)/shard_map/ppermute | solution.py:22
  125.1 5.0 %collective-permute-done.16 = f32[1,16,128]{2,1,0:T(8,128)S(1)} collective-permute-done((f32[1,16,128]{2,1,0:T(8,128)S(1)}, f32[1,16,128]{2,1,0:T(8,128)S(1)}, u32[]{:S(2)}, u32[]{:S(2)}) %collective-permute-start.16) | collective-permute-done | bytes 8224 | tf_op jit(solution)/shard_map/ppermute | solution.py:24
  131.4 3.0 collective-permute-start.19
  136.0 4.8 %collective-permute-start.21 = (f32[1,16,128]{2,1,0:T(8,128)S(1)}, f32[1,16,128]{2,1,0:T(8,128)S(1)}, u32[]{:S(2)}, u32[]{:S(2)}) collective-permute-start(f32[1,16,128]{2,1,0:T(8,128)S(1)} %get-tuple-element.108), channel_id=1, source_target_pairs={{0,2},{2,4},{4,6},{6,8},{8,10},{10,12},{12,14},{1,3},{3,5},{5,7},{... | collective-permute-start | bytes 24584 | tf_op jit(solution)/shard_map/ppermute | solution.py:22
  142.2 4.2 collective-permute-done.20
  147.7 3.0 collective-permute-start.23
  153.6 29.8 %psum.14 = f32[16]{0:T(128)S(1)} all-reduce(f32[16]{0:T(128)S(1)} %compare_select_fusion.1), channel_id=1, replica_groups=mesh['parts'=2,'wide'=8,'narrow'=2] {'wide','narrow'}, use_global_device_ids=true, to_apply=%region_3.4 | all-reduce | flops 16 | bytes 128 | tf_op jit(solution)/shard_map/psum | solution.py:135
  188.0 4.2 collective-permute-done.24
  193.5 3.0 collective-permute-start.27
  201.8 4.2 collective-permute-done.28
  207.3 3.0 collective-permute-start.31
  212.7 1.9 copy.280
  214.6 2.1 broadcast_in_dim.34
  216.7 2.2 copy.281
  219.9 3.0 collective-permute-start.33
  224.5 4.2 collective-permute-done.32
  230.0 3.2 collective-permute-start.35
  235.2 3.0 collective-permute-start.37
  239.8 4.2 collective-permute-done.36
  245.3 3.0 collective-permute-start.39
  249.7 2.8 collective-permute-start.41
  254.1 4.2 collective-permute-done.40
  259.6 3.0 collective-permute-start.43
  263.9 4.8 %collective-permute-start.45 = (f32[1,32,256]{2,1,0:T(8,128)S(1)}, f32[1,32,256]{2,1,0:T(8,128)S(1)}, u32[]{:S(2)}, u32[]{:S(2)}) collective-permute-start(f32[1,32,256]{2,1,0:T(8,128)S(1)} %get-tuple-element.66), channel_id=1, source_target_pairs={{0,2},{2,4},{4,6},{6,8},{8,10},{10,12},{12,14},{1,3},{3,5},{5,7},{... | collective-permute-start | bytes 98312 | tf_op jit(solution)/shard_map/ppermute | solution.py:22
  270.3 4.2 collective-permute-done.44
  275.8 3.0 collective-permute-start.47
  280.7 18.9 %reshape.36 = f32[4,2,16,2,128,2]{5,4,3,2,1,0:T(8,128)} reshape(f32[8,32,256]{2,1,0:T(8,128)} %fusion.58) | data formatting | bytes 524288 | tf_op jit(solution)/shard_map/reshape | solution.py:79
  299.6 7.6 %reduce_sum.67 = f32[4,16,128]{2,1,0:T(8,128)} reduce(f32[4,2,16,2,128,2]{5,4,3,2,1,0:T(8,128)} %reshape.36, f32[]{:T(128)} %constant.45.clone.1), dimensions={1,3,5}, to_apply=%region_5.6 | reduce | flops 57344 | bytes 294916 | tf_op jit(solution)/shard_map/reduce_sum | solution.py:79
  308.0 4.8 %collective-permute-start.49 = (f32[1,16,128]{2,1,0:T(8,128)S(1)}, f32[1,16,128]{2,1,0:T(8,128)S(1)}, u32[]{:S(2)}, u32[]{:S(2)}) collective-permute-start(f32[1,16,128]{2,1,0:T(8,128)S(1)} %get-tuple-element.102), channel_id=1, source_target_pairs={{0,2},{2,4},{4,6},{6,8},{8,10},{10,12},{12,14},{1,3},{3,5},{5,7},{... | collective-permute-start | bytes 24584 | tf_op jit(solution)/shard_map/ppermute | solution.py:22
  314.2 4.2 collective-permute-done.48
  319.7 3.0 collective-permute-start.51
  324.4 2.8 collective-permute-start.53
  328.6 4.2 collective-permute-done.52
  334.1 3.0 collective-permute-start.55
  340.5 30.5 %psum.15 = f32[16]{0:T(128)} all-reduce(f32[16]{0:T(128)} %compare_select_fusion), channel_id=1, replica_groups=mesh['parts'=2,'wide'=8,'narrow'=2] {'wide','narrow'}, use_global_device_ids=true, to_apply=%region_7.8 | all-reduce | flops 16 | bytes 128 | tf_op jit(solution)/shard_map/psum | solution.py:135
  376.2 4.2 collective-permute-done.56
  381.7 3.0 collective-permute-start.59
  390.0 4.2 collective-permute-done.60
  395.5 3.0 collective-permute-start.63
  402.8 2.1 broadcast_in_dim.38
  404.9 2.3 copy.284
  408.3 3.0 collective-permute-start.65
  412.8 4.2 collective-permute-done.64
  418.4 3.0 collective-permute-start.67
  423.6 3.0 collective-permute-start.69
  428.1 4.2 collective-permute-done.68
  433.7 3.0 collective-permute-start.71
  438.2 2.9 collective-permute-start.73
  442.6 4.2 collective-permute-done.72
  448.2 3.0 collective-permute-start.75
  (216 shorter events, 112.8 us)
Async XLA Ops:
  4.6 11.1 %collective-permute-start = (f32[2,32,1024]{2,1,0:T(8,128)S(1)}, f32[2,32,1024]{2,1,0:T(8,128)S(1)}, u32[]{:S(2)}, u32[]{:S(2)}) collective-permute-start(f32[2,32,1024]{2,1,0:T(8,128)S(1)} %get-tuple-element.33), channel_id=1, source_target_pairs={{2,0},{4,2},{6,4},{8,6},{10,8},{12,10},{14,12},{3,1},{5,3},{7,5},{... | collective-permute-start | bytes 786440 | tf_op jit(solution)/shard_map/ppermute | solution.py:24
  5.9 15.6 %collective-permute-start.1 = (f32[2,32,1024]{2,1,0:T(8,128)S(1)}, f32[2,32,1024]{2,1,0:T(8,128)S(1)}, u32[]{:S(2)}, u32[]{:S(2)}) collective-permute-start(f32[2,32,1024]{2,1,0:T(8,128)S(1)} %get-tuple-element.34), channel_id=1, source_target_pairs={{0,2},{2,4},{4,6},{6,8},{8,10},{10,12},{12,14},{1,3},{3,5},{5,7},{... | collective-permute-start | bytes 786440 | tf_op jit(solution)/shard_map/ppermute | solution.py:22
  30.4 32.1 %collective-permute-start.5 = (f32[1,32,256]{2,1,0:T(8,128)}, f32[1,32,256]{2,1,0:T(8,128)S(1)}, u32[]{:S(2)}, u32[]{:S(2)}) collective-permute-start(f32[1,32,256]{2,1,0:T(8,128)} %get-tuple-element.76), channel_id=1, source_target_pairs={{0,2},{2,4},{4,6},{6,8},{8,10},{10,12},{12,14},{1,3},{3,5},{5,7},{... | collective-permute-start | bytes 98312 | tf_op jit(solution)/shard_map/ppermute | solution.py:22
  34.7 27.8 %collective-permute-start.4 = (f32[1,32,256]{2,1,0:T(8,128)}, f32[1,32,256]{2,1,0:T(8,128)}, u32[]{:S(2)}, u32[]{:S(2)}) collective-permute-start(f32[1,32,256]{2,1,0:T(8,128)} %get-tuple-element.77), channel_id=1, source_target_pairs={{2,0},{4,2},{6,4},{8,6},{10,8},{12,10},{14,12},{3,1},{5,3},{7,5},{... | collective-permute-start | bytes 98312 | tf_op jit(solution)/shard_map/ppermute | solution.py:24
  63.4 5.1 %collective-permute-start.6 = (f32[10,1,256]{2,1,0:T(1,128)S(1)}, f32[10,1,256]{2,1,0:T(1,128)S(1)}, u32[]{:S(2)}, u32[]{:S(2)}) collective-permute-start(f32[10,1,256]{2,1,0:T(1,128)S(1)} %get-tuple-element.58), channel_id=1, source_target_pairs={{1,0},{3,2},{5,4},{7,6},{9,8},{11,10},{13,12},{15,14},{17,16},{19,... | collective-permute-start | bytes 30728 | tf_op jit(solution)/shard_map/ppermute | solution.py:24
  64.7 3.8 collective-permute-start.7
  71.2 11.7 %collective-permute-start.13 = (f32[1,32,256]{2,1,0:T(8,128)S(1)}, f32[1,32,256]{2,1,0:T(8,128)S(1)}, u32[]{:S(2)}, u32[]{:S(2)}) collective-permute-start(f32[1,32,256]{2,1,0:T(8,128)S(1)} %get-tuple-element.74), channel_id=1, source_target_pairs={{0,2},{2,4},{4,6},{6,8},{8,10},{10,12},{12,14},{1,3},{3,5},{5,7},{... | collective-permute-start | bytes 98312 | tf_op jit(solution)/shard_map/ppermute | solution.py:22
  75.7 7.2 %collective-permute-start.12 = (f32[1,32,256]{2,1,0:T(8,128)S(1)}, f32[1,32,256]{2,1,0:T(8,128)S(1)}, u32[]{:S(2)}, u32[]{:S(2)}) collective-permute-start(f32[1,32,256]{2,1,0:T(8,128)S(1)} %get-tuple-element.75), channel_id=1, source_target_pairs={{2,0},{4,2},{6,4},{8,6},{10,8},{12,10},{14,12},{3,1},{5,3},{7,5},{... | collective-permute-start | bytes 98312 | tf_op jit(solution)/shard_map/ppermute | solution.py:24
  77.0 10.2 %collective-permute-start.9 = (f32[1,16,128]{2,1,0:T(8,128)S(1)}, f32[1,16,128]{2,1,0:T(8,128)S(1)}, u32[]{:S(2)}, u32[]{:S(2)}) collective-permute-start(f32[1,16,128]{2,1,0:T(8,128)S(1)} %get-tuple-element.112), channel_id=1, source_target_pairs={{0,2},{2,4},{4,6},{6,8},{8,10},{10,12},{12,14},{1,3},{3,5},{5,7},{... | collective-permute-start | bytes 24584 | tf_op jit(solution)/shard_map/ppermute | solution.py:22
  81.6 5.9 %collective-permute-start.8 = (f32[1,16,128]{2,1,0:T(8,128)S(1)}, f32[1,16,128]{2,1,0:T(8,128)S(1)}, u32[]{:S(2)}, u32[]{:S(2)}) collective-permute-start(f32[1,16,128]{2,1,0:T(8,128)S(1)} %get-tuple-element.113), channel_id=1, source_target_pairs={{2,0},{4,2},{6,4},{8,6},{10,8},{12,10},{14,12},{3,1},{5,3},{7,5},{... | collective-permute-start | bytes 24584 | tf_op jit(solution)/shard_map/ppermute | solution.py:24
  82.9 8.3 %collective-permute-start.14 = (f32[10,1,256]{2,1,0:T(1,128)S(1)}, f32[10,1,256]{2,1,0:T(1,128)S(1)}, u32[]{:S(2)}, u32[]{:S(2)}) collective-permute-start(f32[10,1,256]{2,1,0:T(1,128)S(1)} %get-tuple-element.56), channel_id=1, source_target_pairs={{1,0},{3,2},{5,4},{7,6},{9,8},{11,10},{13,12},{15,14},{17,16},{19,... | collective-permute-start | bytes 30728 | tf_op jit(solution)/shard_map/ppermute | solution.py:24
  84.2 7.0 %collective-permute-start.15 = (f32[10,1,256]{2,1,0:T(1,128)S(1)}, f32[10,1,256]{2,1,0:T(1,128)S(1)}, u32[]{:S(2)}, u32[]{:S(2)}) collective-permute-start(f32[10,1,256]{2,1,0:T(1,128)S(1)} %get-tuple-element.57), channel_id=1, source_target_pairs={{0,1},{2,3},{4,5},{6,7},{8,9},{10,11},{12,13},{14,15},{16,17},{18,... | collective-permute-start | bytes 30728 | tf_op jit(solution)/shard_map/ppermute | solution.py:22
  88.1 30.0 %collective-permute-start.11 = (f32[6,1,128]{2,1,0:T(1,128)}, f32[6,1,128]{2,1,0:T(1,128)}, u32[]{:S(2)}, u32[]{:S(2)}) collective-permute-start(f32[6,1,128]{2,1,0:T(1,128)} %get-tuple-element.94), channel_id=1, source_target_pairs={{0,1},{2,3},{4,5},{6,7},{8,9},{10,11},{12,13},{14,15},{16,17},{18,... | collective-permute-start | bytes 9224 | tf_op jit(solution)/shard_map/ppermute | solution.py:22
  90.0 28.2 %collective-permute-start.10 = (f32[6,1,128]{2,1,0:T(1,128)}, f32[6,1,128]{2,1,0:T(1,128)}, u32[]{:S(2)}, u32[]{:S(2)}) collective-permute-start(f32[6,1,128]{2,1,0:T(1,128)} %get-tuple-element.95), channel_id=1, source_target_pairs={{1,0},{3,2},{5,4},{7,6},{9,8},{11,10},{13,12},{15,14},{17,16},{19,... | collective-permute-start | bytes 9224 | tf_op jit(solution)/shard_map/ppermute | solution.py:24
  118.9 6.2 %collective-permute-start.17 = (f32[1,16,128]{2,1,0:T(8,128)S(1)}, f32[1,16,128]{2,1,0:T(8,128)S(1)}, u32[]{:S(2)}, u32[]{:S(2)}) collective-permute-start(f32[1,16,128]{2,1,0:T(8,128)S(1)} %get-tuple-element.110), channel_id=1, source_target_pairs={{0,2},{2,4},{4,6},{6,8},{8,10},{10,12},{12,14},{1,3},{3,5},{5,7},{... | collective-permute-start | bytes 24584 | tf_op jit(solution)/shard_map/ppermute | solution.py:22
  123.8 6.3 %collective-permute-start.16 = (f32[1,16,128]{2,1,0:T(8,128)S(1)}, f32[1,16,128]{2,1,0:T(8,128)S(1)}, u32[]{:S(2)}, u32[]{:S(2)}) collective-permute-start(f32[1,16,128]{2,1,0:T(8,128)S(1)} %get-tuple-element.111), channel_id=1, source_target_pairs={{2,0},{4,2},{6,4},{8,6},{10,8},{12,10},{14,12},{3,1},{5,3},{7,5},{... | collective-permute-start | bytes 24584 | tf_op jit(solution)/shard_map/ppermute | solution.py:24
  130.1 4.3 collective-permute-start.18
  136.0 6.2 %collective-permute-start.21 = (f32[1,16,128]{2,1,0:T(8,128)S(1)}, f32[1,16,128]{2,1,0:T(8,128)S(1)}, u32[]{:S(2)}, u32[]{:S(2)}) collective-permute-start(f32[1,16,128]{2,1,0:T(8,128)S(1)} %get-tuple-element.108), channel_id=1, source_target_pairs={{0,2},{2,4},{4,6},{6,8},{8,10},{10,12},{12,14},{1,3},{3,5},{5,7},{... | collective-permute-start | bytes 24584 | tf_op jit(solution)/shard_map/ppermute | solution.py:22
  140.9 5.5 %collective-permute-start.20 = (f32[1,16,128]{2,1,0:T(8,128)S(1)}, f32[1,16,128]{2,1,0:T(8,128)S(1)}, u32[]{:S(2)}, u32[]{:S(2)}) collective-permute-start(f32[1,16,128]{2,1,0:T(8,128)S(1)} %get-tuple-element.109), channel_id=1, source_target_pairs={{2,0},{4,2},{6,4},{8,6},{10,8},{12,10},{14,12},{3,1},{5,3},{7,5},{... | collective-permute-start | bytes 24584 | tf_op jit(solution)/shard_map/ppermute | solution.py:24
  146.4 4.3 collective-permute-start.22
  147.7 3.8 collective-permute-start.23
  186.7 5.5 %collective-permute-start.24 = (f32[1,16,128]{2,1,0:T(8,128)S(1)}, f32[1,16,128]{2,1,0:T(8,128)S(1)}, u32[]{:S(2)}, u32[]{:S(2)}) collective-permute-start(f32[1,16,128]{2,1,0:T(8,128)S(1)} %get-tuple-element.107), channel_id=1, source_target_pairs={{2,0},{4,2},{6,4},{8,6},{10,8},{12,10},{14,12},{3,1},{5,3},{7,5},{... | collective-permute-start | bytes 24584 | tf_op jit(solution)/shard_map/ppermute | solution.py:24
  192.2 4.3 collective-permute-start.26
  200.5 5.5 %collective-permute-start.28 = (f32[1,16,128]{2,1,0:T(8,128)S(1)}, f32[1,16,128]{2,1,0:T(8,128)S(1)}, u32[]{:S(2)}, u32[]{:S(2)}) collective-permute-start(f32[1,16,128]{2,1,0:T(8,128)S(1)} %get-tuple-element.105), channel_id=1, source_target_pairs={{2,0},{4,2},{6,4},{8,6},{10,8},{12,10},{14,12},{3,1},{5,3},{7,5},{... | collective-permute-start | bytes 24584 | tf_op jit(solution)/shard_map/ppermute | solution.py:24
  206.0 4.3 collective-permute-start.30
  219.9 4.5 %collective-permute-start.33 = (f32[1,32,256]{2,1,0:T(8,128)S(1)}, f32[1,32,256]{2,1,0:T(8,128)S(1)}, u32[]{:S(2)}, u32[]{:S(2)}) collective-permute-start(f32[1,32,256]{2,1,0:T(8,128)S(1)} %get-tuple-element.72), channel_id=1, source_target_pairs={{0,2},{2,4},{4,6},{6,8},{8,10},{10,12},{12,14},{1,3},{3,5},{5,7},{... | collective-permute-start | bytes 98312 | tf_op jit(solution)/shard_map/ppermute | solution.py:22
  222.9 5.8 %collective-permute-start.32 = (f32[1,32,256]{2,1,0:T(8,128)S(1)}, f32[1,32,256]{2,1,0:T(8,128)S(1)}, u32[]{:S(2)}, u32[]{:S(2)}) collective-permute-start(f32[1,32,256]{2,1,0:T(8,128)S(1)} %get-tuple-element.73), channel_id=1, source_target_pairs={{2,0},{4,2},{6,4},{8,6},{10,8},{12,10},{14,12},{3,1},{5,3},{7,5},{... | collective-permute-start | bytes 98312 | tf_op jit(solution)/shard_map/ppermute | solution.py:24
  228.7 4.5 collective-permute-start.34
  230.0 3.8 collective-permute-start.35
  235.2 4.5 %collective-permute-start.37 = (f32[1,32,256]{2,1,0:T(8,128)S(1)}, f32[1,32,256]{2,1,0:T(8,128)S(1)}, u32[]{:S(2)}, u32[]{:S(2)}) collective-permute-start(f32[1,32,256]{2,1,0:T(8,128)S(1)} %get-tuple-element.70), channel_id=1, source_target_pairs={{0,2},{2,4},{4,6},{6,8},{8,10},{10,12},{12,14},{1,3},{3,5},{5,7},{... | collective-permute-start | bytes 98312 | tf_op jit(solution)/shard_map/ppermute | solution.py:22
  238.2 5.8 %collective-permute-start.36 = (f32[1,32,256]{2,1,0:T(8,128)S(1)}, f32[1,32,256]{2,1,0:T(8,128)S(1)}, u32[]{:S(2)}, u32[]{:S(2)}) collective-permute-start(f32[1,32,256]{2,1,0:T(8,128)S(1)} %get-tuple-element.71), channel_id=1, source_target_pairs={{2,0},{4,2},{6,4},{8,6},{10,8},{12,10},{14,12},{3,1},{5,3},{7,5},{... | collective-permute-start | bytes 98312 | tf_op jit(solution)/shard_map/ppermute | solution.py:24
  244.0 4.3 collective-permute-start.38
  245.3 3.8 collective-permute-start.39
  249.7 4.4 collective-permute-start.41
  252.5 5.8 %collective-permute-start.40 = (f32[1,32,256]{2,1,0:T(8,128)S(1)}, f32[1,32,256]{2,1,0:T(8,128)S(1)}, u32[]{:S(2)}, u32[]{:S(2)}) collective-permute-start(f32[1,32,256]{2,1,0:T(8,128)S(1)} %get-tuple-element.69), channel_id=1, source_target_pairs={{2,0},{4,2},{6,4},{8,6},{10,8},{12,10},{14,12},{3,1},{5,3},{7,5},{... | collective-permute-start | bytes 98312 | tf_op jit(solution)/shard_map/ppermute | solution.py:24
  258.3 4.3 collective-permute-start.42
  259.6 3.8 collective-permute-start.43
  263.9 6.3 %collective-permute-start.45 = (f32[1,32,256]{2,1,0:T(8,128)S(1)}, f32[1,32,256]{2,1,0:T(8,128)S(1)}, u32[]{:S(2)}, u32[]{:S(2)}) collective-permute-start(f32[1,32,256]{2,1,0:T(8,128)S(1)} %get-tuple-element.66), channel_id=1, source_target_pairs={{0,2},{2,4},{4,6},{6,8},{8,10},{10,12},{12,14},{1,3},{3,5},{5,7},{... | collective-permute-start | bytes 98312 | tf_op jit(solution)/shard_map/ppermute | solution.py:22
  268.7 5.8 %collective-permute-start.44 = (f32[1,32,256]{2,1,0:T(8,128)S(1)}, f32[1,32,256]{2,1,0:T(8,128)S(1)}, u32[]{:S(2)}, u32[]{:S(2)}) collective-permute-start(f32[1,32,256]{2,1,0:T(8,128)S(1)} %get-tuple-element.67), channel_id=1, source_target_pairs={{2,0},{4,2},{6,4},{8,6},{10,8},{12,10},{14,12},{3,1},{5,3},{7,5},{... | collective-permute-start | bytes 98312 | tf_op jit(solution)/shard_map/ppermute | solution.py:24
  274.5 4.3 collective-permute-start.46
  275.8 3.8 collective-permute-start.47
  308.0 6.1 %collective-permute-start.49 = (f32[1,16,128]{2,1,0:T(8,128)S(1)}, f32[1,16,128]{2,1,0:T(8,128)S(1)}, u32[]{:S(2)}, u32[]{:S(2)}) collective-permute-start(f32[1,16,128]{2,1,0:T(8,128)S(1)} %get-tuple-element.102), channel_id=1, source_target_pairs={{0,2},{2,4},{4,6},{6,8},{8,10},{10,12},{12,14},{1,3},{3,5},{5,7},{... | collective-permute-start | bytes 24584 | tf_op jit(solution)/shard_map/ppermute | solution.py:22
  312.8 5.5 %collective-permute-start.48 = (f32[1,16,128]{2,1,0:T(8,128)S(1)}, f32[1,16,128]{2,1,0:T(8,128)S(1)}, u32[]{:S(2)}, u32[]{:S(2)}) collective-permute-start(f32[1,16,128]{2,1,0:T(8,128)S(1)} %get-tuple-element.103), channel_id=1, source_target_pairs={{2,0},{4,2},{6,4},{8,6},{10,8},{12,10},{14,12},{3,1},{5,3},{7,5},{... | collective-permute-start | bytes 24584 | tf_op jit(solution)/shard_map/ppermute | solution.py:24
  318.4 4.3 collective-permute-start.50
  319.7 3.8 collective-permute-start.51
  324.4 4.2 collective-permute-start.53
  327.2 5.5 %collective-permute-start.52 = (f32[1,16,128]{2,1,0:T(8,128)S(1)}, f32[1,16,128]{2,1,0:T(8,128)S(1)}, u32[]{:S(2)}, u32[]{:S(2)}) collective-permute-start(f32[1,16,128]{2,1,0:T(8,128)S(1)} %get-tuple-element.101), channel_id=1, source_target_pairs={{2,0},{4,2},{6,4},{8,6},{10,8},{12,10},{14,12},{3,1},{5,3},{7,5},{... | collective-permute-start | bytes 24584 | tf_op jit(solution)/shard_map/ppermute | solution.py:24
  332.8 4.3 collective-permute-start.54
  374.8 5.5 %collective-permute-start.56 = (f32[1,16,128]{2,1,0:T(8,128)S(1)}, f32[1,16,128]{2,1,0:T(8,128)S(1)}, u32[]{:S(2)}, u32[]{:S(2)}) collective-permute-start(f32[1,16,128]{2,1,0:T(8,128)S(1)} %get-tuple-element.99), channel_id=1, source_target_pairs={{2,0},{4,2},{6,4},{8,6},{10,8},{12,10},{14,12},{3,1},{5,3},{7,5},{... | collective-permute-start | bytes 24584 | tf_op jit(solution)/shard_map/ppermute | solution.py:24
  380.4 4.3 collective-permute-start.58
  388.6 5.5 %collective-permute-start.60 = (f32[1,16,128]{2,1,0:T(8,128)S(1)}, f32[1,16,128]{2,1,0:T(8,128)S(1)}, u32[]{:S(2)}, u32[]{:S(2)}) collective-permute-start(f32[1,16,128]{2,1,0:T(8,128)S(1)} %get-tuple-element.97), channel_id=1, source_target_pairs={{2,0},{4,2},{6,4},{8,6},{10,8},{12,10},{14,12},{3,1},{5,3},{7,5},{... | collective-permute-start | bytes 24584 | tf_op jit(solution)/shard_map/ppermute | solution.py:24
  394.2 4.3 collective-permute-start.62
  408.3 4.5 %collective-permute-start.65 = (f32[1,32,256]{2,1,0:T(8,128)S(1)}, f32[1,32,256]{2,1,0:T(8,128)S(1)}, u32[]{:S(2)}, u32[]{:S(2)}) collective-permute-start(f32[1,32,256]{2,1,0:T(8,128)S(1)} %get-tuple-element.64), channel_id=1, source_target_pairs={{0,2},{2,4},{4,6},{6,8},{8,10},{10,12},{12,14},{1,3},{3,5},{5,7},{... | collective-permute-start | bytes 98312 | tf_op jit(solution)/shard_map/ppermute | solution.py:22
  411.2 5.8 %collective-permute-start.64 = (f32[1,32,256]{2,1,0:T(8,128)S(1)}, f32[1,32,256]{2,1,0:T(8,128)S(1)}, u32[]{:S(2)}, u32[]{:S(2)}) collective-permute-start(f32[1,32,256]{2,1,0:T(8,128)S(1)} %get-tuple-element.65), channel_id=1, source_target_pairs={{2,0},{4,2},{6,4},{8,6},{10,8},{12,10},{14,12},{3,1},{5,3},{7,5},{... | collective-permute-start | bytes 98312 | tf_op jit(solution)/shard_map/ppermute | solution.py:24
  417.1 4.3 collective-permute-start.66
  418.4 3.8 collective-permute-start.67
  423.6 4.5 %collective-permute-start.69 = (f32[1,32,256]{2,1,0:T(8,128)S(1)}, f32[1,32,256]{2,1,0:T(8,128)S(1)}, u32[]{:S(2)}, u32[]{:S(2)}) collective-permute-start(f32[1,32,256]{2,1,0:T(8,128)S(1)} %get-tuple-element.62), channel_id=1, source_target_pairs={{0,2},{2,4},{4,6},{6,8},{8,10},{10,12},{12,14},{1,3},{3,5},{5,7},{... | collective-permute-start | bytes 98312 | tf_op jit(solution)/shard_map/ppermute | solution.py:22
  426.5 5.8 %collective-permute-start.68 = (f32[1,32,256]{2,1,0:T(8,128)S(1)}, f32[1,32,256]{2,1,0:T(8,128)S(1)}, u32[]{:S(2)}, u32[]{:S(2)}) collective-permute-start(f32[1,32,256]{2,1,0:T(8,128)S(1)} %get-tuple-element.63), channel_id=1, source_target_pairs={{2,0},{4,2},{6,4},{8,6},{10,8},{12,10},{14,12},{3,1},{5,3},{7,5},{... | collective-permute-start | bytes 98312 | tf_op jit(solution)/shard_map/ppermute | solution.py:24
  432.4 4.3 collective-permute-start.70
  433.7 3.8 collective-permute-start.71
  438.2 4.5 collective-permute-start.73
  441.1 5.8 %collective-permute-start.72 = (f32[1,32,256]{2,1,0:T(8,128)S(1)}, f32[1,32,256]{2,1,0:T(8,128)S(1)}, u32[]{:S(2)}, u32[]{:S(2)}) collective-permute-start(f32[1,32,256]{2,1,0:T(8,128)S(1)} %get-tuple-element.61), channel_id=1, source_target_pairs={{2,0},{4,2},{6,4},{8,6},{10,8},{12,10},{14,12},{3,1},{5,3},{7,5},{... | collective-permute-start | bytes 98312 | tf_op jit(solution)/shard_map/ppermute | solution.py:24
  446.9 4.3 collective-permute-start.74
  448.2 3.8 collective-permute-start.75
  (28 other events, 367.8 us)
where the time goes:
time: 458 us; the launch traced here: 453 us
  starting transfers between devices  169 us (37%)
  waiting for transfers between devices  90.4 us (20%)
  local copies, waits for them, and re-layouts  76.9 us (17%)
  blocking collectives  60.3 us (13%)
  other arithmetic  54.8 us (12%)
    ppermute x38, starting transfers between devices, padded_2(): lax.ppermute(tail, axis, [(i, (i + 1) % count) for i in range(ends)])  120 us
    ppermute x38, waiting for transfers between devices, padded_2(): lax.ppermute(head, axis, [((i + 1) % count, i) for i in range(ends)])  70.5 us
    psum x2, blocking collectives, vcycle(): lax.psum(jnp.where(slot_ids == slot, leftover, 0.0), ('wide', 'narrow'))  60.3 us
    reshape x3, local copies, waits for them, and re-layouts, coarsen(): values.reshape(first // 2, 2, second // 2, 2, third // 2, 2)  56.6 us
    ppermute x38, starting transfers between devices, padded_2(): lax.ppermute(head, axis, [((i + 1) % count, i) for i in range(ends)])  49 us
    reduce_sum x3, other arithmetic, coarsen(): values.reshape(first // 2, 2, second // 2, 2, third // 2, 2)  22.1 us
    ppermute x38, waiting for transfers between devices, padded_2(): lax.ppermute(tail, axis, [(i, (i + 1) % count) for i in range(ends)])  19.9 us
  transfers between devices with their start and end apart: 76, of which 41 were waited for; matrix products, arithmetic and copies ran while one was open for 12% of the time, Pallas kernels for 0%

commit v1 on v0

v1 whole, which is shorter than its diff:
```python
import functools

import jax
import jax.numpy as jnp
from jax import lax
from jax.experimental import pallas as pl
from jax.experimental.pallas import tpu as pltpu
from jax.sharding import PartitionSpec as P

MESH = pl.DeviceIdType.MESH
f32 = jnp.float32
bf16 = jnp.bfloat16

cheb_mid = 1.125
cheb_half = 0.875
first_rho = cheb_half / cheb_mid
second_rho = 1.0 / (2.0 * cheb_mid / cheb_half - first_rho)
step_gain = 2.0 * second_rho / cheb_half
carry_gain = second_rho * first_rho
inv_mid = 1.0 / cheb_mid


def split3(a):
    hi = a.astype(bf16)
    rest = a - hi.astype(f32)
    mid = rest.astype(bf16)
    low = (rest - mid.astype(f32)).astype(bf16)
    return hi, mid, low


def permuted(a, perm):
    parts = [jnp.dot(s, perm, preferred_element_type=f32) for s in split3(a)]
    return parts[0] + (parts[1] + parts[2])


def kernel(n, nb, state_in, k_in, dir_in, w_in, inv_in, hess_out, inc_out, stage, t_s, t_k, t_c, t_w, s_r, k_r, c_r, w_r,
           czi, czo, cyi, cyo, cx, dia, inv, b_r, x1_r, x2_r, xa, xb, upd, kc, ccx, ccy, ccz, diac, invc, g_r, y1, y2_r,
           ya, yb, updc, tot, corr, adj, o_inc, o_hess, r_inc, r_hess, send_sem, recv_sem):
    wide = lax.axis_index("wide")
    core = lax.axis_index("narrow")
    n_wide = n // 2
    p = 2 * wide + core
    other = 1 - core
    rows = 32
    half = 16
    depth = 128

    def dev(q):
        q = jnp.clip(q, 0, n - 1)
        return {"wide": q // 2, "narrow": q % 2}

    barrier = pltpu.get_barrier_semaphore()

    def greet(d, _):
        q = lax.rem(p + d, n)
        pl.semaphore_signal(barrier, inc=1, device_id={"wide": q // 2, "narrow": q % 2}, device_id_type=MESH)
        return 0

    lax.fori_loop(1, n, greet, 0)

    counter = [0]

    def remote(src, dst, target):
        i = counter[0]
        counter[0] += 1
        return pltpu.make_async_remote_copy(src_ref=src, dst_ref=dst, send_sem=send_sem.at[i], recv_sem=recv_sem.at[i],
                                            device_id=target, device_id_type=MESH)

    has = {-1: p >= 1, 1: p <= n - 2, -2: p >= 2, 2: p <= n - 3}
    chip = {-1: wide >= 1, 1: wide <= n_wide - 2}

    class Halo:
        def __init__(self, moves):
            self.moves = [(off, remote(src, dst, dev(p + off))) for off, src, dst in moves]

        def start(self):
            for off, copy in self.moves:
                pl.when(has[off])(copy.start)

        def recv(self):
            for off, copy in self.moves:
                pl.when(has[-off])(copy.wait_recv)

        def sent(self):
            for off, copy in self.moves:
                pl.when(has[off])(copy.wait_send)

    zf = jnp.zeros((4, rows, depth), f32)
    zc = jnp.zeros((rows, depth), f32)

    @pl.when(p == 0)
    def _():
        for l in (0, 1):
            k_r[l] = zf
            s_r[l] = zf
            c_r[l] = zf
            for cyc in (0, 1):
                b_r[cyc, l] = zf
                x1_r[cyc, l] = zf
                x2_r[cyc, l] = zf
            adj[l] = zf
        for l in (0, 1, 2):
            kc[l] = zc
            for cyc in (0, 1):
                g_r[cyc, l] = zc
                y2_r[cyc, l] = zc

    @pl.when(p == n - 1)
    def _():
        for l in (6, 7):
            k_r[l] = zf
            s_r[l] = zf
            c_r[l] = zf
            for cyc in (0, 1):
                b_r[cyc, l] = zf
                x1_r[cyc, l] = zf
                x2_r[cyc, l] = zf
            adj[l] = zf
        for l in (5, 6, 7):
            kc[l] = zc
            for cyc in (0, 1):
                g_r[cyc, l] = zc
                y2_r[cyc, l] = zc

    @pl.when(p == 1)
    def _():
        kc[0] = zc
        for cyc in (0, 1):
            y2_r[cyc, 0] = zc

    @pl.when(p == n - 2)
    def _():
        kc[7] = zc
        for cyc in (0, 1):
            y2_r[cyc, 7] = zc

    row_i = lax.broadcasted_iota(jnp.int32, (256, 256), 0)
    col_i = lax.broadcasted_iota(jnp.int32, (256, 256), 1)
    apart = jnp.where(row_i == jnp.where(col_i < 128, 2 * col_i, 2 * col_i - 255), 1.0, 0.0).astype(bf16)
    together = jnp.where(col_i == jnp.where(row_i < 128, 2 * row_i, 2 * row_i - 255), 1.0, 0.0).astype(bf16)

    mine = pl.multiple_of(half * core, half)
    theirs = pl.multiple_of(half * other, half)

    def planes(values, t_ref, region):
        flat = permuted(values.reshape(256, 256), apart)
        stage[0] = flat[:, :128].reshape(8, 32, 128)
        stage[1] = flat[:, 128:].reshape(8, 32, 128)
        for yp in range(2):
            for zp in range(2):
                t_ref[:, 2 * yp + zp] = stage[zp, :, pl.ds(yp, half, stride=2), :]
        region[pl.ds(2 - 2 * core, 6), :, pl.ds(mine, half), :] = t_ref[pl.ds(2 * core, 6)]

    planes(k_in[...], t_k, k_r)
    planes(k_in[...] * dir_in[...], t_c, c_r)
    planes(state_in[...], t_s, s_r)

    def first(t_ref, region, deep):
        i = counter[0]
        counter[0] += 6
        partner = pltpu.make_async_remote_copy(
            src_ref=t_ref.at[pl.ds(2 * other, 6)], dst_ref=region.at[pl.ds(2 - 2 * other, 6), :, pl.ds(mine, half), :],
            send_sem=send_sem.at[i], recv_sem=recv_sem.at[i], device_id={"narrow": other}, device_id_type=MESH)
        left = right = None
        if deep:
            left = pltpu.make_async_remote_copy(
                src_ref=t_ref.at[pl.ds(0, deep)], dst_ref=region.at[pl.ds(6, deep), :, pl.ds(mine, half), :],
                send_sem=send_sem.at[i + 1], recv_sem=recv_sem.at[i + 2 + core],
                device_id={"wide": jnp.maximum(wide - 1, 0), "narrow": 1}, device_id_type=MESH)
            right = pltpu.make_async_remote_copy(
                src_ref=t_ref.at[pl.ds(8 - deep, deep)], dst_ref=region.at[pl.ds(2 - deep, deep), :, pl.ds(mine, half), :],
                send_sem=send_sem.at[i + 2], recv_sem=recv_sem.at[i + 2 + core],
                device_id={"wide": jnp.minimum(wide + 1, n_wide - 1), "narrow": 0}, device_id_type=MESH)

        def start():
            if deep:
                pl.when(chip[-1])(left.start)
                pl.when(chip[1])(right.start)
            partner.start()

        def recv():
            partner.wait_recv()
            if deep:
                arrives = ((core == 0) & chip[-1]) | ((core == 1) & chip[1])

                @pl.when(arrives)
                def _():
                    for c in (0, 1):
                        at = jnp.where(core == 0, 2 - deep, 6)
                        pltpu.make_async_copy(t_ref.at[pl.ds(0, deep)],
                                              region.at[pl.ds(at, deep), :, pl.ds(half * c, half), :],
                                              recv_sem.at[i + 2 + c]).wait()

        def sent():
            partner.wait_send()
            if deep:
                pl.when(chip[-1])(left.wait_send)
                pl.when(chip[1])(right.wait_send)

        return start, recv, sent

    firsts = [first(t_k, k_r, 2), first(t_c, c_r, 1), first(t_s, s_r, 1)]
    weight_move = first(t_w, w_r, 0)

    pl.semaphore_wait(barrier, n - 1)
    for move in firsts:
        move[0]()
    planes(w_in[...], t_w, w_r)
    weight_move[0]()

    lane_i = lax.broadcasted_iota(jnp.int32, (rows, depth), 1)
    sub_i = lax.broadcasted_iota(jnp.int32, (rows, depth), 0)
    lane_first, lane_last = lane_i == 0, lane_i == depth - 1
    sub_first, sub_last = sub_i == 0, sub_i == rows - 1

    def after(v, axis):
        return pltpu.roll(v, v.shape[axis] - 1, axis)

    def before(v, axis):
        return pltpu.roll(v, 1, axis)

    def after0(v, axis):
        return jnp.where(sub_last if axis == 0 else lane_last, 0.0, after(v, axis))

    def before0(v, axis):
        return jnp.where(sub_first if axis == 0 else lane_first, 0.0, before(v, axis))

    pairs = ((1, ((0, 1), (2, 3))), (0, ((0, 2), (1, 3))))

    def four(ref, *index):
        return [ref[(*index, q)] for q in range(4)]

    def faces(c):
        inner, outer, around = {}, {}, [None] * 4
        for axis, sets in pairs:
            inner[axis], outer[axis] = [], []
            last = sub_last if axis == 0 else lane_last
            for ev, od in sets:
                inner[axis].append(0.5 * (c[ev] + c[od]))
                outer[axis].append(jnp.where(last, 0.0, 0.5 * (c[od] + after(c[ev], axis))))
                se = c[od] + before0(c[od], axis)
                so = c[ev] + after0(c[ev], axis)
                around[ev] = se if around[ev] is None else around[ev] + se
                around[od] = so if around[od] is None else around[od] + so
        return inner, outer, around

    def within(v, inner, outer):
        acc = [None] * 4
        for axis, sets in pairs:
            for i, (ev, od) in enumerate(sets):
                fi, fo = inner[axis][i], outer[axis][i]
                se = fi * v[od] + before(fo * v[od], axis)
                so = fi * v[ev] + fo * after(v[ev], axis)
                acc[ev] = se if acc[ev] is None else acc[ev] + se
                acc[od] = so if acc[od] is None else acc[od] + so
        return acc

    def loop(low, high, body):
        def step(l, _):
            body(l)
            return 0

        lax.fori_loop(low, high, step, 0)

    def cross(l):
        for q in range(4):
            cx[l, q] = 0.5 * (k_r[l, q] + k_r[l + 1, q])

    def prepare(l):
        c = four(k_r, l)
        inner, outer, around = faces(c)
        for i in range(2):
            czi[l, i], czo[l, i] = inner[1][i], outer[1][i]
            cyi[l, i], cyo[l, i] = inner[0][i], outer[0][i]
        layer = 4 * p - 2 + l
        inside = (layer >= 0) & (layer < 4 * n)
        for q in range(4):
            d = 3.0 * c[q] + 0.5 * (around[q] + k_r[l - 1, q] + k_r[l + 1, q])
            dia[l, q] = d
            inv[l, q] = jnp.where(inside, 1.0 / jnp.where(inside, d, 1.0), 0.0)

    def applied(ref, l, *index):
        v = four(ref, *index, l)
        inner = {1: [czi[l, 0], czi[l, 1]], 0: [cyi[l, 0], cyi[l, 1]]}
        outer = {1: [czo[l, 0], czo[l, 1]], 0: [cyo[l, 0], cyo[l, 1]]}
        acc = within(v, inner, outer)
        out = []
        for q in range(4):
            beside = acc[q] + (cx[l, q] * ref[(*index, l + 1, q)] + cx[l - 1, q] * ref[(*index, l - 1, q)])
            out.append(dia[l, q] * v[q] - beside)
        return out

    def source(l):
        c = four(c_r, l)
        inner, outer, around = faces(c)
        v = four(s_r, l)
        acc = within(v, inner, outer)
        for q in range(4):
            up, down = c_r[l + 1, q], c_r[l - 1, q]
            d = 3.0 * c[q] + 0.5 * (around[q] + up + down)
            beside = acc[q] + 0.5 * ((c[q] + up) * s_r[l + 1, q] + (c[q] + down) * s_r[l - 1, q])
            b_r[0, l, q] = beside - d * v[q]

    def start_smooth(l, cyc):
        for q in range(4):
            x1_r[cyc, l, q] = inv[l, q] * b_r[cyc, l, q] * inv_mid

    def end_smooth(l, cyc):
        ax = applied(x1_r, l, cyc)
        for q in range(4):
            x1 = x1_r[cyc, l, q]
            x2_r[cyc, l, q] = x1 + (carry_gain * x1 + step_gain * inv[l, q] * (b_r[cyc, l, q] - ax[q]))

    def whole_sum(v):
        return jnp.sum(jnp.sum(v, axis=0, keepdims=True), axis=1, keepdims=True)

    def coarse_prepare(l):
        c = kc[l]
        up, down = kc[l + 1], kc[l - 1]
        ccy[l] = jnp.where(sub_last, 0.0, 0.125 * (c + after(c, 0)))
        ccz[l] = jnp.where(lane_last, 0.0, 0.125 * (c + after(c, 1)))
        around = after0(c, 0) + before0(c, 0) + after0(c, 1) + before0(c, 1) + up + down
        d = 0.25 * (3.0 * c + 0.5 * around)
        layer = 2 * p - 3 + l
        inside = (layer >= 0) & (layer < 2 * n)
        diac[l] = d
        invc[l] = jnp.where(inside, 1.0 / jnp.where(inside, d, 1.0), 0.0)

    def coarse_cross(l):
        ccx[l] = 0.125 * (kc[l] + kc[l + 1])

    def coarse_applied(get, l):
        v = get(l)
        fy, fz = ccy[l], ccz[l]
        beside = fy * after(v, 0) + before(fy * v, 0) + fz * after(v, 1) + before(fz * v, 1)
        beside = beside + (ccx[l] * get(l + 1) + ccx[l - 1] * get(l - 1))
        return diac[l] * v - beside

    def home(o_ref, t_ref):
        return remote(o_ref.at[:, :, pl.ds(theirs, half), :], t_ref.at[pl.ds(4 * core, 4)], {"narrow": other})

    def assemble(o_ref, t_ref, out_ref):
        t_ref[pl.ds(4 * core, 4)] = o_ref[:, :, pl.ds(mine, half), :]
        for yp in range(2):
            for zp in range(2):
                stage[zp, :, pl.ds(yp, half, stride=2), :] = t_ref[:, 2 * yp + zp]
        flat = jnp.concatenate([stage[0].reshape(256, 128), stage[1].reshape(256, 128)], axis=1)
        out_ref[...] = permuted(flat, together).reshape(8, 32, 256)

    for move in firsts:
        move[1]()

    for j in (0, 1):
        total = None
        for l in (2 + 2 * j, 3 + 2 * j):
            for q in range(4):
                total = k_r[l, q] if total is None else total + k_r[l, q]
        kc[3 + j] = 0.125 * total
    halo_kc = Halo([(-1, kc.at[pl.ds(3, 2)], kc.at[pl.ds(5, 2)]), (1, kc.at[pl.ds(3, 2)], kc.at[pl.ds(1, 2)]),
                    (-2, kc.at[3], kc.at[7]), (2, kc.at[4], kc.at[0])])
    pending = []

    loop(2, 6, prepare)
    loop(2, 6, source)
    half_row = sub_i < half

    for cyc in (0, 1):
        if cyc == 1:
            def adjoint_source(l):
                for q in range(4):
                    b_r[1, l, q] = -(w_r[l, q] * o_inc[l - 2, q])

            weight_move[1]()
            loop(2, 6, adjoint_source)
        loop(2, 6, functools.partial(start_smooth, cyc=cyc))
        halo_b = Halo([(-1, b_r.at[cyc, 2], b_r.at[cyc, 6]), (1, b_r.at[cyc, 5], b_r.at[cyc, 1]),
                       (-1, x1_r.at[cyc, 3], x1_r.at[cyc, 7]), (1, x1_r.at[cyc, 4], x1_r.at[cyc, 0])])
        halo_b.start()
        pending.append(halo_b)
        if cyc == 0:
            halo_kc.start()
            pending.append(halo_kc)
            loop(0, 7, cross)
            prepare(1)
            prepare(6)
        else:
            inc_move = home(o_inc, r_inc)
            inc_move.start()
        loop(3, 5, functools.partial(end_smooth, cyc=cyc))
        halo_b.recv()
        start_smooth(1, cyc)
        start_smooth(6, cyc)
        loop(1, 3, functools.partial(end_smooth, cyc=cyc))
        loop(5, 7, functools.partial(end_smooth, cyc=cyc))
        halo_x2 = Halo([(-1, x2_r.at[cyc, 3], x2_r.at[cyc, 7]), (1, x2_r.at[cyc, 4], x2_r.at[cyc, 0])])

        def restrict(j):
            total = None
            for i in (0, 1):
                l = 2 * j - 4 + i
                ax = applied(x2_r, l, cyc)
                for q in range(4):
                    r = b_r[cyc, l, q] - ax[q]
                    total = r if total is None else total + r
            g_r[cyc, j] = 0.125 * total

        loop(3, 5, restrict)
        halo_g = Halo([(-1, g_r.at[cyc, pl.ds(3, 2)], g_r.at[cyc, pl.ds(5, 2)]),
                       (1, g_r.at[cyc, pl.ds(3, 2)], g_r.at[cyc, pl.ds(1, 2)])])
        halo_g.start()
        halo_x2.start()
        pending += [halo_g, halo_x2]
        if cyc == 0:
            halo_kc.recv()
            loop(0, 7, coarse_cross)
            loop(1, 7, coarse_prepare)
        else:
            inc_move.wait_recv()
            assemble(o_inc, r_inc, inc_out)
        halo_g.recv()

        def coarse_start(l):
            y1[l] = invc[l] * g_r[cyc, l] * inv_mid

        def coarse_end(l):
            ay = coarse_applied(lambda i: y1[i], l)
            v = y1[l]
            y2_r[cyc, l] = v + (carry_gain * v + step_gain * invc[l] * (g_r[cyc, l] - ay))

        loop(1, 7, coarse_start)
        loop(2, 6, coarse_end)
        halo_y = Halo([(-1, y2_r.at[cyc, 4], y2_r.at[cyc, 6]), (1, y2_r.at[cyc, 3], y2_r.at[cyc, 1]),
                       (-2, y2_r.at[cyc, 3], y2_r.at[cyc, 7]), (2, y2_r.at[cyc, 4], y2_r.at[cyc, 0])])
        left_over = None
        for l in (3, 4):
            r = g_r[cyc, l] - coarse_applied(lambda i: y2_r[cyc, i], l)
            left_over = r if left_over is None else left_over + r
        low = whole_sum(left_over[:half])
        high = whole_sum(left_over[half:])
        slots = lax.broadcasted_iota(jnp.int32, (1, tot.shape[-1]), 1)
        tot[cyc, 0] = jnp.where(slots == 2 * wide, low, jnp.where(slots == 2 * wide + 1, high, 0.0))
        sem_at = counter[0]
        counter[0] += 1

        def total_copy(d):
            q = lax.rem(p + d, n)
            return pltpu.make_async_remote_copy(
                src_ref=tot.at[cyc, 0], dst_ref=tot.at[cyc, d], send_sem=send_sem.at[sem_at],
                recv_sem=recv_sem.at[sem_at], device_id={"wide": q // 2, "narrow": q % 2}, device_id_type=MESH)

        loop(1, n, lambda d: total_copy(d).start())
        halo_y.start()
        pending.append(halo_y)
        halo_y.recv()
        everyone = tot.at[cyc, pl.ds(1, n - 1)]
        pltpu.make_async_copy(everyone, everyone, recv_sem.at[sem_at]).wait()
        pltpu.make_async_copy(everyone, everyone, send_sem.at[sem_at]).wait()
        totals = jnp.sum(tot[cyc], axis=0)[:, :nb]
        for i in range(3):
            at = jnp.clip(wide + i - 1, 0, n_wide - 1)
            ends = wide + i - 1
            inside = (ends >= 0) & (ends < n_wide)
            values = []
            for h in range(2):
                row = inv_in[pl.ds(2 * at + h, 1), :]
                values.append(jnp.sum(row * totals, axis=1, keepdims=True))
            corr[i] = jnp.where(inside, jnp.where(half_row, values[0], values[1]), 0.0)

        def coarse_add(l):
            ya[l] = y2_r[cyc, l] + corr[(2 * core + 1 + l) // 4]

        def coarse_third(l):
            e = invc[l] * (g_r[cyc, l] - coarse_applied(lambda i: ya[i], l)) * inv_mid
            updc[l] = e
            yb[l] = ya[l] + e

        def coarse_fourth(l):
            r = g_r[cyc, l] - coarse_applied(lambda i: yb[i], l)
            y1[l] = yb[l] + (carry_gain * updc[l] + step_gain * invc[l] * r)

        loop(0, 8, coarse_add)
        loop(1, 7, coarse_third)
        loop(2, 6, coarse_fourth)
        halo_x2.recv()

        def prolong(j):
            y = y1[j]
            for i in (0, 1):
                l = 2 * j - 4 + i
                for q in range(4):
                    xa[l, q] = x2_r[cyc, l, q] + y

        def third(l):
            ax = applied(xa, l)
            for q in range(4):
                e = inv[l, q] * (b_r[cyc, l, q] - ax[q]) * inv_mid
                upd[l, q] = e
                xb[l, q] = xa[l, q] + e

        def fourth(l):
            ax = applied(xb, l)
            for q in range(4):
                r = b_r[cyc, l, q] - ax[q]
                out = xb[l, q] + (carry_gain * upd[l, q] + step_gain * inv[l, q] * r)
                if cyc == 0:
                    o_inc[l - 2, q] = out
                else:
                    adj[l, q] = out

        loop(2, 6, prolong)
        loop(1, 7, third)
        loop(2, 6, fourth)

    halo_adj = Halo([(-1, adj.at[2], adj.at[6]), (1, adj.at[5], adj.at[1])])
    halo_adj.start()
    pending.append(halo_adj)

    def hessian(l):
        s, a = four(s_r, l), four(adj, l)
        acc = [(s[q] - s_r[l + 1, q]) * (a[q] - adj[l + 1, q]) + (s[q] - s_r[l - 1, q]) * (a[q] - adj[l - 1, q])
               for q in range(4)]
        for axis, sets in pairs:
            first_one = sub_first if axis == 0 else lane_first
            for ev, od in sets:
                i = (s[ev] - s[od]) * (a[ev] - a[od])
                o = (s[od] - after0(s[ev], axis)) * (a[od] - after0(a[ev], axis))
                acc[ev] = acc[ev] + i + jnp.where(first_one, s[ev] * a[ev], before(o, axis))
                acc[od] = acc[od] + i + o
        for q in range(4):
            o_hess[l - 2, q] = 0.5 * k_r[l, q] * acc[q]

    loop(3, 5, hessian)
    halo_adj.recv()
    hessian(2)
    hessian(5)

    hess_move = home(o_hess, r_hess)
    hess_move.start()
    hess_move.wait_recv()
    assemble(o_hess, r_hess, hess_out)
    for halo in pending:
        halo.sent()
    for move in firsts + [weight_move]:
        move[2]()
    inc_move.wait_send()
    hess_move.wait_send()


def shards(n, state, permeability, direction, obs_weight, coarse_inverse):
    nb = coarse_inverse.shape[0]
    width = max(128, nb)
    fine = pltpu.VMEM((8, 4, 32, 128), f32)
    fine2 = pltpu.VMEM((2, 8, 4, 32, 128), f32)
    face = pltpu.VMEM((8, 2, 32, 128), f32)
    turned = pltpu.VMEM((8, 4, 16, 128), f32)
    coarse = pltpu.VMEM((8, 32, 128), f32)
    coarse2 = pltpu.VMEM((2, 8, 32, 128), f32)
    owned = pltpu.VMEM((4, 4, 32, 128), f32)
    vmem = pl.BlockSpec(memory_space=pltpu.VMEM)
    scratch = [pltpu.VMEM((2, 8, 32, 128), f32)] + [turned] * 4 + [fine] * 4 + [face] * 4 + [fine] * 3
    scratch += [fine2] * 3 + [fine] * 3
    scratch += [coarse] * 6 + [coarse2, coarse, coarse2] + [coarse] * 3
    scratch += [pltpu.VMEM((2, n, 1, width), f32), pltpu.VMEM((3, 32, 128), f32), fine, owned, owned, turned, turned]
    scratch += [pltpu.SemaphoreType.DMA((72,)), pltpu.SemaphoreType.DMA((72,))]
    shape = jax.ShapeDtypeStruct(state.shape, f32)
    return pl.pallas_call(
        functools.partial(kernel, n, nb),
        out_shape=(shape, shape),
        in_specs=[vmem] * 5,
        out_specs=(vmem, vmem),
        scratch_shapes=scratch,
        compiler_params=pltpu.CompilerParams(collective_id=0, has_side_effects=True, vmem_limit_bytes=40 * 1024 * 1024),
    )(state, permeability, direction, obs_weight, coarse_inverse)


def solution(mesh):
    field = P(("parts", "wide"), "narrow", None)
    return jax.shard_map(
        functools.partial(shards, mesh.shape["wide"] * mesh.shape["narrow"]),
        mesh=mesh,
        in_specs=(field, field, field, field, P("parts", None)),
        out_specs=(field, field),
        check_vma=False,
    )
```

time: 458 us -> 54.9 us (0.12); the launches traced: 453 us -> 54.6 us
  starting transfers between devices: 169 us -> 0 us
  waiting for transfers between devices: 90.4 us -> 0 us
  local copies, waits for them, and re-layouts: 76.9 us -> 5.9 us
  blocking collectives: 60.3 us -> 0 us
  other arithmetic: 54.8 us -> 0 us
  Pallas kernels: 0 us -> 48.1 us
    ppermute x76 -> x0, starting transfers between devices: 169 us -> none  [the longest x38 120 us: padded_2(): lax.ppermute(tail, axis, [(i, (i + 1) % count) for i in range(ends)])]
    ppermute x76 -> x0, waiting for transfers between devices: 90.4 us -> none  [the longest x38 70.5 us: padded_2(): lax.ppermute(head, axis, [((i + 1) % count, i) for i in range(ends)])]
    reshape x7 -> x0, local copies, waits for them, and re-layouts: 64.9 us -> none  [the longest x3 56.6 us: coarsen(): values.reshape(first // 2, 2, second // 2, 2, third // 2, 2)]
    psum x2 -> x0, blocking collectives: 60.3 us -> none  [vcycle(): lax.psum(jnp.where(slot_ids == slot, leftover, 0.0), ('wide', 'narrow'))]
    pallas_call x0 -> x1, Pallas kernels: none -> 48.1 us  [shards(): pl.pallas_call(functools.partial(kernel, n, nb), out_shape=(shape, shape)...]
    reduce_sum x7 -> x0, other arithmetic: 27.5 us -> none  [the longest x3 22.1 us: coarsen(): values.reshape(first // 2, 2, second // 2, 2, third // 2, 2)]
    add x15 -> x0, other arithmetic: 16.4 us -> none  [the longest x4 5.51 us: smooth_from(): iterate = start + update]
    broadcast_in_dim x6 -> x0, local copies, waits for them, and re-layouts: 5.56 us -> none  [refine(): return jnp.repeat(jnp.repeat(jnp.repeat(values, 2, 0), 2, 1), 2, 2)]
  transfers between devices with their start and end apart: 76 -> 0, of which waited for: 41 -> 0; matrix products, arithmetic and copies ran while one was open for 12% -> 0% of each run, Pallas kernels for 0% -> 0%
where the time goes in v1:
time: 54.9 us; the launch traced here: 54.6 us
  Pallas kernels  48.1 us (88%)
  local copies, waits for them, and re-layouts  5.9 us (11%)
  between operations  0.65 us (1%)
    pallas_call x1, Pallas kernels, shards(): pl.pallas_call(functools.partial(kernel, n, nb), out_shape=(shape, shape)...  48.1 us
    unnamed x12, local copies, waits for them, and re-layouts  5.9 us

profile of v1, /device:TPU:0, one launch (start us, length us, event | category | flops | bytes accessed | tf_op | source)
XLA Modules:
  0.0 54.6 jit_solution(13770277313317319558)
XLA Ops:
  0.6 0.0 copy-start
  0.6 0.9 %copy-done = f32[8,32,256]{2,1,0:T(8,128)S(1)} copy-done((f32[8,32,256]{2,1,0:T(8,128)S(1)}, f32[8,32,256]{2,1,0:T(8,128)}, u32[]{:S(2)}) %copy-start) | copy-done | bytes 262168
  1.6 0.0 copy-start.1
  1.6 0.9 %copy-done.1 = f32[8,32,256]{2,1,0:T(8,128)S(1)} copy-done((f32[8,32,256]{2,1,0:T(8,128)S(1)}, f32[8,32,256]{2,1,0:T(8,128)}, u32[]{:S(2)}) %copy-start.1) | copy-done | bytes 262168
  2.5 0.0 copy-start.2
  2.5 0.9 %copy-done.2 = f32[8,32,256]{2,1,0:T(8,128)S(1)} copy-done((f32[8,32,256]{2,1,0:T(8,128)S(1)}, f32[8,32,256]{2,1,0:T(8,128)}, u32[]{:S(2)}) %copy-start.2) | copy-done | bytes 262168
  3.5 0.0 copy-start.3
  3.5 0.9 %copy-done.3 = f32[8,32,256]{2,1,0:T(8,128)S(1)} copy-done((f32[8,32,256]{2,1,0:T(8,128)S(1)}, f32[8,32,256]{2,1,0:T(8,128)}, u32[]{:S(2)}) %copy-start.3) | copy-done | bytes 262168
  4.4 0.0 copy-start.4
  4.4 0.7 %copy-done.4 = f32[16,16]{1,0:T(8,128)S(1)} copy-done((f32[16,16]{1,0:T(8,128)S(1)}, f32[16,16]{1,0:T(8,128)}, u32[]{:S(2)}) %copy-start.4) | copy-done | bytes 1048
  5.1 48.1 %shard_map.68 = (f32[8,32,256]{2,1,0:T(8,128)S(1)}, f32[8,32,256]{2,1,0:T(8,128)S(1)}) custom-call(f32[8,32,256]{2,1,0:T(8,128)S(1)} %copy-done, f32[8,32,256]{2,1,0:T(8,128)S(1)} %copy-done.1, f32[8,32,256]{2,1,0:T(8,128)S(1)} %copy-done.2, f32[8,32,256]{2,1,0:T(8,128)S(1)} %copy-done.3, f32[16,16]{1,0:T(8,128)S(1)} %copy-done.4), custom_call_target="tpu_custom_call" | custom-call | tf_op jit(solution)/shard_map/pallas_call | solution.py:566
  53.2 0.7 %copy.9 = f32[8,32,256]{2,1,0:T(8,128)} copy(f32[8,32,256]{2,1,0:T(8,128)S(1)} %get-tuple-element.4) | data formatting | bytes 524288
  53.9 0.7 %copy.10 = f32[8,32,256]{2,1,0:T(8,128)} copy(f32[8,32,256]{2,1,0:T(8,128)S(1)} %get-tuple-element.5) | data formatting | bytes 524288
Async XLA Ops:
  0.6 1.0 %copy-start = (f32[8,32,256]{2,1,0:T(8,128)S(1)}, f32[8,32,256]{2,1,0:T(8,128)}, u32[]{:S(2)}) copy-start(f32[8,32,256]{2,1,0:T(8,128)} %state_in.1) | copy-start | bytes 786436
  1.6 0.9 %copy-start.1 = (f32[8,32,256]{2,1,0:T(8,128)S(1)}, f32[8,32,256]{2,1,0:T(8,128)}, u32[]{:S(2)}) copy-start(f32[8,32,256]{2,1,0:T(8,128)} %k_in.1) | copy-start | bytes 786436
  2.5 0.9 %copy-start.2 = (f32[8,32,256]{2,1,0:T(8,128)S(1)}, f32[8,32,256]{2,1,0:T(8,128)}, u32[]{:S(2)}) copy-start(f32[8,32,256]{2,1,0:T(8,128)} %dir_in.1) | copy-start | bytes 786436
  3.5 0.9 %copy-start.3 = (f32[8,32,256]{2,1,0:T(8,128)S(1)}, f32[8,32,256]{2,1,0:T(8,128)}, u32[]{:S(2)}) copy-start(f32[8,32,256]{2,1,0:T(8,128)} %w_in.1) | copy-start | bytes 786436
  4.4 0.7 %copy-start.4 = (f32[16,16]{1,0:T(8,128)S(1)}, f32[16,16]{1,0:T(8,128)}, u32[]{:S(2)}) copy-start(f32[16,16]{1,0:T(8,128)} %inv_in.1) | copy-start | bytes 3076

commit v2 on v1

--- a/solution.py
+++ b/solution.py
@@ -33,9 +33,9 @@
     return parts[0] + (parts[1] + parts[2])
 
 
-def kernel(n, nb, state_in, k_in, dir_in, w_in, inv_in, hess_out, inc_out, stage, t_s, t_k, t_c, t_w, s_r, k_r, c_r, w_r,
+def kernel(n, nb, state_hbm, k_hbm, dir_hbm, w_hbm, inv_hbm, hess_out, inc_out, state_in, k_in, dir_in, w_in, inv_in, stage, t_s, t_k, t_c, t_w, s_r, k_r, c_r, w_r,
            czi, czo, cyi, cyo, cx, dia, inv, b_r, x1_r, x2_r, xa, xb, upd, kc, ccx, ccy, ccz, diac, invc, g_r, y1, y2_r,
-           ya, yb, updc, tot, corr, adj, o_inc, o_hess, r_inc, r_hess, send_sem, recv_sem):
+           ya, yb, updc, tot, corr, adj, o_inc, o_hess, r_inc, r_hess, send_sem, recv_sem, load_sem):
     wide = lax.axis_index("wide")
     core = lax.axis_index("narrow")
     n_wide = n // 2
@@ -48,6 +48,12 @@
     def dev(q):
         q = jnp.clip(q, 0, n - 1)
         return {"wide": q // 2, "narrow": q % 2}
+
+    sources = (k_hbm, dir_hbm, state_hbm, w_hbm, inv_hbm)
+    loads = [pltpu.make_async_copy(src, dst, load_sem.at[i])
+             for i, (src, dst) in enumerate(zip(sources, (k_in, dir_in, state_in, w_in, inv_in)))]
+    for load in loads:
+        load.start()
 
     barrier = pltpu.get_barrier_semaphore()
 
@@ -151,11 +157,14 @@
                 t_ref[:, 2 * yp + zp] = stage[zp, :, pl.ds(yp, half, stride=2), :]
         region[pl.ds(2 - 2 * core, 6), :, pl.ds(mine, half), :] = t_ref[pl.ds(2 * core, 6)]
 
+    loads[0].wait()
     planes(k_in[...], t_k, k_r)
+    loads[1].wait()
     planes(k_in[...] * dir_in[...], t_c, c_r)
+    loads[2].wait()
     planes(state_in[...], t_s, s_r)
 
-    def first(t_ref, region, deep):
+    def first(t_ref, region, deep, skip=0):
         i = counter[0]
         counter[0] += 6
         partner = pltpu.make_async_remote_copy(
@@ -164,11 +173,11 @@
         left = right = None
         if deep:
             left = pltpu.make_async_remote_copy(
-                src_ref=t_ref.at[pl.ds(0, deep)], dst_ref=region.at[pl.ds(6, deep), :, pl.ds(mine, half), :],
+                src_ref=t_ref.at[pl.ds(skip, deep)], dst_ref=region.at[pl.ds(6 + skip, deep), :, pl.ds(mine, half), :],
                 send_sem=send_sem.at[i + 1], recv_sem=recv_sem.at[i + 2 + core],
                 device_id={"wide": jnp.maximum(wide - 1, 0), "narrow": 1}, device_id_type=MESH)
             right = pltpu.make_async_remote_copy(
-                src_ref=t_ref.at[pl.ds(8 - deep, deep)], dst_ref=region.at[pl.ds(2 - deep, deep), :, pl.ds(mine, half), :],
+                src_ref=t_ref.at[pl.ds(8 - skip - deep, deep)], dst_ref=region.at[pl.ds(2 - skip - deep, deep), :, pl.ds(mine, half), :],
                 send_sem=send_sem.at[i + 2], recv_sem=recv_sem.at[i + 2 + core],
                 device_id={"wide": jnp.minimum(wide + 1, n_wide - 1), "narrow": 0}, device_id_type=MESH)
 
@@ -176,35 +185,41 @@
             if deep:
                 pl.when(chip[-1])(left.start)
                 pl.when(chip[1])(right.start)
-            partner.start()
+            if not skip:
+                partner.start()
 
         def recv():
-            partner.wait_recv()
+            if not skip:
+                partner.wait_recv()
             if deep:
                 arrives = ((core == 0) & chip[-1]) | ((core == 1) & chip[1])
 
                 @pl.when(arrives)
                 def _():
                     for c in (0, 1):
-                        at = jnp.where(core == 0, 2 - deep, 6)
+                        at = jnp.where(core == 0, 2 - skip - deep, 6 + skip)
                         pltpu.make_async_copy(t_ref.at[pl.ds(0, deep)],
                                               region.at[pl.ds(at, deep), :, pl.ds(half * c, half), :],
                                               recv_sem.at[i + 2 + c]).wait()
 
         def sent():
-            partner.wait_send()
+            if not skip:
+                partner.wait_send()
             if deep:
                 pl.when(chip[-1])(left.wait_send)
                 pl.when(chip[1])(right.wait_send)
 
         return start, recv, sent
 
-    firsts = [first(t_k, k_r, 2), first(t_c, c_r, 1), first(t_s, s_r, 1)]
+    firsts = [first(t_k, k_r, 1), first(t_c, c_r, 1), first(t_s, s_r, 1)]
     weight_move = first(t_w, w_r, 0)
+    second_k = first(t_k, k_r, 1, 1)
 
     pl.semaphore_wait(barrier, n - 1)
     for move in firsts:
         move[0]()
+    loads[3].wait()
+    loads[4].wait()
     planes(w_in[...], t_w, w_r)
     weight_move[0]()
 
@@ -358,7 +373,9 @@
         kc[3 + j] = 0.125 * total
     halo_kc = Halo([(-1, kc.at[pl.ds(3, 2)], kc.at[pl.ds(5, 2)]), (1, kc.at[pl.ds(3, 2)], kc.at[pl.ds(1, 2)]),
                     (-2, kc.at[3], kc.at[7]), (2, kc.at[4], kc.at[0])])
-    pending = []
+    second_k[0]()
+    halo_kc.start()
+    pending = [halo_kc]
 
     loop(2, 6, prepare)
     loop(2, 6, source)
@@ -373,26 +390,33 @@
             weight_move[1]()
             loop(2, 6, adjoint_source)
         loop(2, 6, functools.partial(start_smooth, cyc=cyc))
-        halo_b = Halo([(-1, b_r.at[cyc, 2], b_r.at[cyc, 6]), (1, b_r.at[cyc, 5], b_r.at[cyc, 1]),
-                       (-1, x1_r.at[cyc, 3], x1_r.at[cyc, 7]), (1, x1_r.at[cyc, 4], x1_r.at[cyc, 0])])
+        halo_b = Halo([(-1, b_r.at[cyc, 2], b_r.at[cyc, 6]), (1, b_r.at[cyc, 5], b_r.at[cyc, 1])])
+        halo_x1 = Halo([(-1, x1_r.at[cyc, 3], x1_r.at[cyc, 7]), (1, x1_r.at[cyc, 4], x1_r.at[cyc, 0])])
         halo_b.start()
-        pending.append(halo_b)
+        halo_x1.start()
+        pending += [halo_b, halo_x1]
         if cyc == 0:
-            halo_kc.start()
-            pending.append(halo_kc)
-            loop(0, 7, cross)
-            prepare(1)
-            prepare(6)
+            loop(1, 6, cross)
         else:
             inc_move = home(o_inc, r_inc)
             inc_move.start()
         loop(3, 5, functools.partial(end_smooth, cyc=cyc))
+        if cyc == 0:
+            second_k[1]()
+            cross(0)
+            cross(6)
+            prepare(1)
+            prepare(6)
         halo_b.recv()
         start_smooth(1, cyc)
         start_smooth(6, cyc)
-        loop(1, 3, functools.partial(end_smooth, cyc=cyc))
-        loop(5, 7, functools.partial(end_smooth, cyc=cyc))
         halo_x2 = Halo([(-1, x2_r.at[cyc, 3], x2_r.at[cyc, 7]), (1, x2_r.at[cyc, 4], x2_r.at[cyc, 0])])
+        end_smooth(2, cyc)
+        end_smooth(5, cyc)
+        halo_x1.recv()
+        halo_x2.start()
+        end_smooth(1, cyc)
+        end_smooth(6, cyc)
 
         def restrict(j):
             total = None
@@ -408,7 +432,6 @@
         halo_g = Halo([(-1, g_r.at[cyc, pl.ds(3, 2)], g_r.at[cyc, pl.ds(5, 2)]),
                        (1, g_r.at[cyc, pl.ds(3, 2)], g_r.at[cyc, pl.ds(1, 2)])])
         halo_g.start()
-        halo_x2.start()
         pending += [halo_g, halo_x2]
         if cyc == 0:
             halo_kc.recv()
@@ -540,7 +563,7 @@
     assemble(o_hess, r_hess, hess_out)
     for halo in pending:
         halo.sent()
-    for move in firsts + [weight_move]:
+    for move in firsts + [weight_move, second_k]:
         move[2]()
     inc_move.wait_send()
     hess_move.wait_send()
@@ -557,19 +580,20 @@
     coarse2 = pltpu.VMEM((2, 8, 32, 128), f32)
     owned = pltpu.VMEM((4, 4, 32, 128), f32)
     vmem = pl.BlockSpec(memory_space=pltpu.VMEM)
-    scratch = [pltpu.VMEM((2, 8, 32, 128), f32)] + [turned] * 4 + [fine] * 4 + [face] * 4 + [fine] * 3
+    scratch = [pltpu.VMEM(state.shape, f32)] * 4 + [pltpu.VMEM(coarse_inverse.shape, f32)]
+    scratch += [pltpu.VMEM((2, 8, 32, 128), f32)] + [turned] * 4 + [fine] * 4 + [face] * 4 + [fine] * 3
     scratch += [fine2] * 3 + [fine] * 3
     scratch += [coarse] * 6 + [coarse2, coarse, coarse2] + [coarse] * 3
     scratch += [pltpu.VMEM((2, n, 1, width), f32), pltpu.VMEM((3, 32, 128), f32), fine, owned, owned, turned, turned]
-    scratch += [pltpu.SemaphoreType.DMA((72,)), pltpu.SemaphoreType.DMA((72,))]
+    scratch += [pltpu.SemaphoreType.DMA((72,)), pltpu.SemaphoreType.DMA((72,)), pltpu.SemaphoreType.DMA((5,))]
     shape = jax.ShapeDtypeStruct(state.shape, f32)
     return pl.pallas_call(
         functools.partial(kernel, n, nb),
         out_shape=(shape, shape),
-        in_specs=[vmem] * 5,
+        in_specs=[pl.BlockSpec(memory_space=pltpu.HBM)] * 5,
         out_specs=(vmem, vmem),
         scratch_shapes=scratch,
-        compiler_params=pltpu.CompilerParams(collective_id=0, has_side_effects=True, vmem_limit_bytes=40 * 1024 * 1024),
+        compiler_params=pltpu.CompilerParams(collective_id=0, has_side_effects=True, vmem_limit_bytes=60 * 1024 * 1024),
     )(state, permeability, direction, obs_weight, coarse_inverse)
 
 

time: 54.9 us -> 52.1 us (0.949)
  local copies, waits for them, and re-layouts: 5.9 us -> 2.42 us
  Pallas kernels: 48.1 us -> 48.9 us
    unnamed x12 -> x4, local copies, waits for them, and re-layouts: 5.9 us -> 2.42 us
    pallas_call x1, Pallas kernels: 48.1 us -> 48.9 us  [shards(): pl.pallas_call(functools.partial(kernel, n, nb), out_shape=(shape, shape)...]
where the time goes in v2:
time: 52.1 us; the launch traced here: 52 us
  Pallas kernels  48.9 us (94%)
  local copies, waits for them, and re-layouts  2.42 us (5%)
  between operations  0.65 us (1%)
    pallas_call x1, Pallas kernels, shards(): pl.pallas_call(functools.partial(kernel, n, nb), out_shape=(shape, shape)...  48.9 us
    unnamed x4, local copies, waits for them, and re-layouts  2.42 us

profile of v2, /device:TPU:0, one launch (start us, length us, event | category | flops | bytes accessed | tf_op | source)
XLA Modules:
  0.0 52.0 jit_solution(1751924500830196649)
XLA Ops:
  0.6 48.9 %shard_map.68 = (f32[8,32,256]{2,1,0:T(8,128)}, f32[8,32,256]{2,1,0:T(8,128)}) custom-call(f32[8,32,256]{2,1,0:T(8,128)} %state_hbm.1, f32[8,32,256]{2,1,0:T(8,128)} %k_hbm.1, f32[8,32,256]{2,1,0:T(8,128)} %dir_hbm.1, f32[8,32,256]{2,1,0:T(8,128)} %w_hbm.1, f32[16,16]{1,0:T(8,128)} %inv_hbm.1), custom_call_target="tpu_custom_call" | custom-call | tf_op jit(solution)/shard_map/pallas_call | solution.py:590
  49.5 0.0 copy-start
  49.6 1.7 %copy.9 = f32[8,32,256]{2,1,0:T(8,128)} copy(f32[8,32,256]{2,1,0:T(8,128)} %get-tuple-element.4) | data formatting | bytes 524288
  51.3 0.0 copy-done
  51.3 0.7 %copy.10 = f32[8,32,256]{2,1,0:T(8,128)} copy(f32[8,32,256]{2,1,0:T(8,128)S(1)} %copy-done) | data formatting | bytes 524288
Async XLA Ops:
  49.5 1.7 %copy-start = (f32[8,32,256]{2,1,0:T(8,128)S(1)}, f32[8,32,256]{2,1,0:T(8,128)}, u32[]{:S(2)}) copy-start(f32[8,32,256]{2,1,0:T(8,128)} %get-tuple-element.5) | copy-start | bytes 786436

commit v3 on v2

--- a/solution.py
+++ b/solution.py
@@ -164,11 +164,12 @@
     loads[2].wait()
     planes(state_in[...], t_s, s_r)
 
-    def first(t_ref, region, deep, skip=0):
+    def first(t_ref, region, deep, extra, skip=0):
         i = counter[0]
         counter[0] += 6
         partner = pltpu.make_async_remote_copy(
-            src_ref=t_ref.at[pl.ds(2 * other, 6)], dst_ref=region.at[pl.ds(2 - 2 * other, 6), :, pl.ds(mine, half), :],
+            src_ref=t_ref.at[pl.ds((4 - extra) * other, 4 + extra)],
+            dst_ref=region.at[pl.ds(2 - extra * other, 4 + extra), :, pl.ds(mine, half), :],
             send_sem=send_sem.at[i], recv_sem=recv_sem.at[i], device_id={"narrow": other}, device_id_type=MESH)
         left = right = None
         if deep:
@@ -211,9 +212,9 @@
 
         return start, recv, sent
 
-    firsts = [first(t_k, k_r, 1), first(t_c, c_r, 1), first(t_s, s_r, 1)]
-    weight_move = first(t_w, w_r, 0)
-    second_k = first(t_k, k_r, 1, 1)
+    firsts = [first(t_k, k_r, 1, 2), first(t_c, c_r, 1, 1), first(t_s, s_r, 1, 1)]
+    weight_move = first(t_w, w_r, 0, 0)
+    second_k = first(t_k, k_r, 1, 0, 1)
 
     pl.semaphore_wait(barrier, n - 1)
     for move in firsts:
@@ -221,7 +222,6 @@
     loads[3].wait()
     loads[4].wait()
     planes(w_in[...], t_w, w_r)
-    weight_move[0]()
 
     lane_i = lax.broadcasted_iota(jnp.int32, (rows, depth), 1)
     sub_i = lax.broadcasted_iota(jnp.int32, (rows, depth), 0)
@@ -434,6 +434,7 @@
         halo_g.start()
         pending += [halo_g, halo_x2]
         if cyc == 0:
+            weight_move[0]()
             halo_kc.recv()
             loop(0, 7, coarse_cross)
             loop(1, 7, coarse_prepare)

time: 52.1 us -> 52.1 us (level)
  no operation moved by 1% of the time
where the time goes in v3:
time: 52.1 us; the launch traced here: 52 us
  Pallas kernels  48.9 us (94%)
  local copies, waits for them, and re-layouts  2.42 us (5%)
  between operations  0.65 us (1%)
    pallas_call x1, Pallas kernels, shards(): pl.pallas_call(functools.partial(kernel, n, nb), out_shape=(shape, shape)...  48.9 us
    unnamed x4, local copies, waits for them, and re-layouts  2.42 us

profile of v3, /device:TPU:0, one launch (start us, length us, event | category | flops | bytes accessed | tf_op | source)
XLA Modules:
  0.0 52.0 jit_solution(17706187512535319287)
XLA Ops:
  0.6 48.9 %shard_map.68 = (f32[8,32,256]{2,1,0:T(8,128)}, f32[8,32,256]{2,1,0:T(8,128)}) custom-call(f32[8,32,256]{2,1,0:T(8,128)} %state_hbm.1, f32[8,32,256]{2,1,0:T(8,128)} %k_hbm.1, f32[8,32,256]{2,1,0:T(8,128)} %dir_hbm.1, f32[8,32,256]{2,1,0:T(8,128)} %w_hbm.1, f32[16,16]{1,0:T(8,128)} %inv_hbm.1), custom_call_target="tpu_custom_call" | custom-call | tf_op jit(solution)/shard_map/pallas_call | solution.py:591
  49.6 0.0 copy-start
  49.6 1.7 %copy.9 = f32[8,32,256]{2,1,0:T(8,128)} copy(f32[8,32,256]{2,1,0:T(8,128)} %get-tuple-element.4) | data formatting | bytes 524288
  51.3 0.0 copy-done
  51.3 0.7 %copy.10 = f32[8,32,256]{2,1,0:T(8,128)} copy(f32[8,32,256]{2,1,0:T(8,128)S(1)} %copy-done) | data formatting | bytes 524288
Async XLA Ops:
  49.6 1.7 %copy-start = (f32[8,32,256]{2,1,0:T(8,128)S(1)}, f32[8,32,256]{2,1,0:T(8,128)}, u32[]{:S(2)}) copy-start(f32[8,32,256]{2,1,0:T(8,128)} %get-tuple-element.5) | copy-start | bytes 786436
